TPU v7x, 32 devices: a whole 2x2x4 slice. The times are simulated.
32 devices in a mesh: depth: 8 (over y, x, core), filt: 4 (over z).
Axes of the slice: x: 2, y: 2, z: 4, core: 2. Of those that a mesh axis runs over, the one named last changes fastest.
Arguments:
- upper_level: bfloat16 [64, 32, 16, 256], P(None, 'depth', 'filt'), may hold values from -6 to 6
- stride_weight: bfloat16 [8, 128, 64], P(None, 'filt'), may hold values from -0.25 to 0.25
- middle_weight: bfloat16 [27, 128, 128], P(None, 'filt'), may hold values from -0.109375 to 0.109375
- last_weight: bfloat16 [27, 128, 128], P(None, 'filt'), may hold values from -0.109375 to 0.109375
- cotangent: bfloat16 [128, 16, 8, 128], P('filt', 'depth'), may hold values from -0.046875 to 0.046875
Outputs:
- result: bfloat16 [128, 16, 8, 128], P('filt', 'depth')
- grad_stride: float32 [8, 128, 64], P(None, 'filt')
- grad_middle: float32 [27, 128, 128], P(None, 'filt')
- grad_last: float32 [27, 128, 128], P(None, 'filt')
All inputs are finite; a program needn't handle non-finite values.
Results may differ from a plain program's by a relative error of at most 0.0059.
Values may be sent and summed in bfloat16 or wider, within the bound.
A program may use at most 64 MiB of HBM per device.

v0:
```python
import functools

import jax
import jax.numpy as jnp
from jax import lax
from jax.experimental import pallas as pl
from jax.experimental.pallas import tpu as pltpu
from jax.sharding import PartitionSpec as P

F32 = jnp.float32
BF16 = jnp.bfloat16
MESH = pl.DeviceIdType.MESH
NEAR = [(z, y) for z in (-1, 0, 1) for y in (-1, 0, 1) if (z, y) != (0, 0)]


def dot(left, right, dims):
    return lax.dot_general(left, right, ((dims[:1], dims[1:]), ((), ())), preferred_element_type=F32)


def silu_slope(value):
    sigma = 1.0 / (1.0 + jnp.exp(-value))
    return sigma * (1.0 + value * (1.0 - sigma))


def silu(value):
    return value / (1.0 + jnp.exp(-value))


def kernel(
    n, m, dl, hl, W,
    up, sw, wm, wl, cot,
    res, gs, gm, gl,
    SW, WM, WL, XL, XM, XG, XD, U, pre_l, pre_m, R,
    pb_s, r1_s, z_s, zr_s, dr_s,
    pb_m, r1_m, z_m, zr_m, dr_m,
    pb_l, r1_l, z_l, zr_l, dr_l,
    near_send, near_recv, swap_send, swap_recv,
    wz_send, wz_recv, wp_send, wp_recv,
    s1_send, s1_recv, s2_send, s2_recv, s3_send, s3_recv, s4_send, s4_recv,
):
    d, f = lax.axis_index("depth"), lax.axis_index("filt")
    oc, C = cot.shape[1], WM.shape[1]
    CI = up.shape[1]
    hb = oc // 2
    half = lax.rem(d, 2)
    mate = d + 1 - 2 * half
    cols = hl * W

    for X in (XL, XM, XG, XD):
        X[...] = jnp.zeros_like(X)

    def at(steps_d, steps_f):
        return (lax.rem(d + steps_d + n, n), lax.rem(f + steps_f + m, m))

    barrier = pltpu.get_barrier_semaphore()
    greet = [(0, k) for k in range(1, m)] + [(y, z) for z, y in NEAR if y != 0]
    greet += [(2 * j, 0) for j in range(1, n // 2)]
    for step in greet:
        pl.semaphore_signal(barrier, inc=1, device_id=at(*step), device_id_type=MESH)
    pl.semaphore_wait(barrier, len(greet))

    def remote(src, dst, send, recv, where):
        return pltpu.make_async_remote_copy(
            src_ref=src, dst_ref=dst, send_sem=send, recv_sem=recv, device_id=where, device_id_type=MESH
        )

    def mul(value, by):
        return pl.multiple_of(value * by, by)

    own = pl.ds(mul(f, oc), oc)
    sends = []
    for k in range(1, m):
        where = at(0, k)
        copy = remote(sw, SW.at[own], swap_send.at[0, k - 1], swap_recv.at[0, k - 1], where)
        copy.start()
        sends.append(copy)

    def weight_out(index, src, dst):
        copies = []
        part = pl.ds(mul(half, hb), hb)
        spot = pl.ds(pl.multiple_of(f * oc + half * hb, hb), hb)
        for k in range(1, m):
            copy = remote(
                src.at[:, part], dst.at[:, spot], wz_send.at[index, k - 1], wz_recv.at[index, k - 1], at(0, k)
            )
            copy.start()
            copies.append(copy)
        return copies

    cot_copies = []
    wm_copies = weight_out(0, wm, WM)
    for k in range(1, m):
        where = at(0, k)
        copy = remote(
            cot.at[:, :, pl.ds(mul(where[1], cols), cols)],
            XG.at[pl.ds(1, dl), own, pl.ds(W, cols)],
            swap_send.at[1, k - 1],
            swap_recv.at[1, k - 1],
            where,
        )
        copy.start()
        cot_copies.append(copy)
    wl_copies = weight_out(1, wl, WL)

    SW[own, :] = sw[...]
    WM[:, own, :] = wm[...]
    WL[:, own, :] = wl[...]
    XG[pl.ds(1, dl), own, pl.ds(W, cols)] = cot[:, :, pl.ds(mul(f, cols), cols)]

    line = lax.broadcasted_iota(jnp.int32, (2 * W, 2 * W), 0)
    column = lax.broadcasted_iota(jnp.int32, (2 * W, 2 * W), 1)
    wanted = jnp.where(column < W, 2 * column, 2 * (column - W) + 1)
    pick = jnp.where(line == wanted, 1.0, 0.0).astype(BF16)
    for plane in range(2 * dl):
        for row in range(2 * hl):
            both = dot(up[plane * 2 * hl + row], pick, (1, 0)).astype(BF16)
            tap = 4 * (plane % 2) + 2 * (row % 2)
            place = ((plane // 2) * hl + row // 2) * W
            U[tap * CI : (tap + 1) * CI, place : place + W] = both[:, :W]
            U[(tap + 1) * CI : (tap + 2) * CI, place : place + W] = both[:, W:]

    lane = lax.rem(lax.broadcasted_iota(jnp.int32, (C, cols), 1), W)

    def before(value):
        return jnp.where(lane == 0, 0.0, pltpu.roll(value, 1, 1))

    def after(value):
        return jnp.where(lane == W - 1, 0.0, pltpu.roll(value, cols - 1, 1))

    def near_copy(index, X, number):
        z, y = NEAR[number]
        src_p, dst_p = {0: ((1, dl), (1, dl)), 1: ((dl, 1), (0, 1)), -1: ((1, 1), (dl + 1, 1))}[y]
        src_c, dst_c = {
            0: ((W, cols), (W, cols)),
            1: ((cols, W), (0, W)),
            -1: ((W, W), (cols + W, W)),
        }[z]
        return remote(
            X.at[pl.ds(*src_p), :, pl.ds(*src_c)],
            X.at[pl.ds(*dst_p), :, pl.ds(*dst_c)],
            near_send.at[index, number],
            near_recv.at[index, number],
            at(y, z),
        )

    def inside(z, y):
        return (f + z >= 0) & (f + z < m) & (d + y >= 0) & (d + y < n)

    def near_start(index, X):
        for number, (z, y) in enumerate(NEAR):
            @pl.when(inside(z, y))
            def _():
                near_copy(index, X, number).start()

    def near_wait(index, X):
        for number, (z, y) in enumerate(NEAR):
            @pl.when(inside(-z, -y))
            def _():
                near_copy(index, X, number).wait_recv()

    def near_end(index, X):
        for number, (z, y) in enumerate(NEAR):
            @pl.when(inside(z, y))
            def _():
                near_copy(index, X, number).wait_send()

    def conv(X, weights, plane):
        total = jnp.zeros((3 * C, cols), F32)
        for a in range(3):
            for b in range(3):
                tap = 9 * a + 3 * b
                left = weights[tap : tap + 3].reshape(3 * C, C)
                total += dot(left, X[plane + a, :, b * W : b * W + cols], (1, 0))
        return before(total[:C]) + total[C : 2 * C] + after(total[2 * C :])

    def conv_back(X, weights, plane):
        parts = []
        for c in range(3):
            total = jnp.zeros((C, cols), F32)
            for a in range(3):
                for b in range(3):
                    right = X[plane + 2 - a, :, (2 - b) * W : (2 - b) * W + cols]
                    total += dot(weights[9 * a + 3 * b + c], right, (0, 0))
            parts.append(total)
        return after(parts[0]) + parts[1] + before(parts[2])

    def weight_grad(D, X, out):
        left = []
        for plane in range(dl):
            value = D[plane + 1, :, W : W + cols]
            wide = value.astype(F32)
            left.append(jnp.concatenate([after(wide).astype(BF16), value, before(wide).astype(BF16)], axis=0))
        for a in range(3):
            for b in range(3):
                total = dot(left[0], X[a, :, b * W : b * W + cols], (1, 1))
                for plane in range(1, dl):
                    total += dot(left[plane], X[plane + a, :, b * W : b * W + cols], (1, 1))
                tap = 9 * a + 3 * b
                out[tap : tap + 3] = total.astype(BF16).reshape(3, m, 2, hb, C)

    def sum_1(index, pb, r1):
        copy = remote(pb.at[:, :, 1 - half], r1, s1_send.at[index], s1_recv.at[index], (mate, f))
        copy.start()
        return [copy]

    def sum_2(index, copies, pb, r1, z, zr):
        copies[0].wait()

        def body(t, carry):
            z[t] = (pb[t, :, half].astype(F32) + r1[t].astype(F32)).astype(BF16)
            return carry

        lax.fori_loop(0, pb.shape[0], body, 0)
        out = []
        for k in range(1, m):
            where = at(0, k)
            copy = remote(
                z.at[:, where[1]], zr.at[k - 1], s2_send.at[index, k - 1], s2_recv.at[index, k - 1], where
            )
            copy.start()
            out.append(copy)
        return out

    def sum_3(index, copies, pb, r1, z, zr, dr):
        for copy in copies:
            copy.wait()
        slot = d // 2

        def body(t, carry):
            total = pb[t, f, half].astype(F32) + r1[t, f].astype(F32)
            for k in range(m - 1):
                total += zr[k, t].astype(F32)
            dr[slot, t] = total.astype(BF16)
            return carry

        lax.fori_loop(0, pb.shape[0], body, 0)
        out = []
        for j in range(1, n // 2):
            copy = remote(
                dr.at[slot], dr.at[slot], s3_send.at[index, j - 1], s3_recv.at[index, j - 1], at(2 * j, 0)
            )
            copy.start()
            out.append(copy)
        return out

    def sum_4(index, copies, dr, out):
        for copy in copies:
            copy.wait()
        part = pl.ds(mul(half, hb), hb)

        def body(t, carry):
            total = dr[0, t].astype(F32)
            for j in range(1, n // 2):
                total += dr[j, t].astype(F32)
            out[t, part, :] = total
            return carry

        lax.fori_loop(0, out.shape[0], body, 0)
        copy = remote(out.at[:, part], out.at[:, part], s4_send.at[index], s4_recv.at[index], (mate, f))
        copy.start()
        return [copy]

    def weight_pass(index, copies, dst):
        out = []
        for k in range(1, m):
            copies[k - 1].wait()
            spot = pl.ds(pl.multiple_of(lax.rem(f - k + m, m) * oc + half * hb, hb), hb)
            copy = remote(
                dst.at[:, spot], dst.at[:, spot], wp_send.at[index, k - 1], wp_recv.at[index, k - 1], (mate, f)
            )
            copy.start()
            out.append(copy)
        return out

    def flat(X, plane):
        return X[plane + 1, :, W : W + cols]

    for copy in sends:
        copy.wait()
    for plane in range(dl):
        value = dot(SW[...], U[:, plane * cols : (plane + 1) * cols], (1, 0))
        pre_l[plane] = value
        XL[plane + 1, :, W : W + cols] = silu(value).astype(BF16)
    near_start(0, XL)
    wm_pass = weight_pass(0, wm_copies, WM)
    for copy in cot_copies:
        copy.wait()
    near_start(1, XG)
    near_wait(0, XL)
    for copy in wm_pass:
        copy.wait()
    for plane in range(dl):
        value = conv(XL, WM, plane)
        pre_m[plane] = value
        XM[plane + 1, :, W : W + cols] = silu(value).astype(BF16)
    near_start(2, XM)
    wl_pass = weight_pass(1, wl_copies, WL)
    near_wait(1, XG)
    for copy in wl_pass:
        copy.wait()

    for plane in range(dl):
        value = conv_back(XG, WL, plane) * silu_slope(pre_m[plane])
        XD[plane + 1, :, W : W + cols] = value.astype(BF16)
    near_start(3, XD)
    weight_grad(XD, XL, pb_m)
    sum_m = sum_1(0, pb_m, r1_m)
    near_wait(2, XM)
    weight_grad(XG, XM, pb_l)
    sum_l = sum_1(1, pb_l, r1_l)
    sum_m = sum_2(0, sum_m, pb_m, r1_m, z_m, zr_m)
    near_wait(3, XD)
    left = []
    for plane in range(dl):
        value = conv_back(XD, WM, plane) * silu_slope(pre_l[plane])
        left.append(value.astype(BF16))
    total = dot(left[0], U[:, :cols], (1, 1))
    for plane in range(1, dl):
        total += dot(left[plane], U[:, plane * cols : (plane + 1) * cols], (1, 1))
    pb_s[...] = total.astype(BF16).reshape(pb_s.shape)
    sum_s = sum_1(2, pb_s, r1_s)
    sum_l = sum_2(1, sum_l, pb_l, r1_l, z_l, zr_l)
    sum_s = sum_2(2, sum_s, pb_s, r1_s, z_s, zr_s)

    for plane in range(dl):
        R[plane] = conv(XM, WL, plane).astype(BF16)
    out_spot = pl.ds(mul(f, cols), cols)
    out_copies = []
    for k in range(1, m):
        where = at(0, k)
        copy = remote(
            R.at[:, pl.ds(mul(where[1], oc), oc)],
            res.at[:, :, out_spot],
            swap_send.at[2, k - 1],
            swap_recv.at[2, k - 1],
            where,
        )
        copy.start()
        out_copies.append(copy)
    res[:, :, out_spot] = R[:, own]

    sum_m = sum_3(0, sum_m, pb_m, r1_m, z_m, zr_m, dr_m)
    sum_l = sum_3(1, sum_l, pb_l, r1_l, z_l, zr_l, dr_l)
    sum_s = sum_3(2, sum_s, pb_s, r1_s, z_s, zr_s, dr_s)
    sum_m = sum_4(0, sum_m, dr_m, gm)
    sum_l = sum_4(1, sum_l, dr_l, gl)
    sum_s = sum_4(2, sum_s, dr_s, gs)
    for copy in out_copies + sum_m + sum_l + sum_s:
        copy.wait()
    for index, X in enumerate((XL, XG, XM, XD)):
        near_end(index, X)


def per_device(n, m, upper_level, stride_weight, middle_weight, last_weight, cotangent):
    oc, dl, H, W = cotangent.shape
    hl = H // m
    C, CI = oc * m, upper_level.shape[0]
    T = middle_weight.shape[0]
    hb = oc // 2
    up = upper_level.transpose(1, 2, 0, 3).reshape(4 * dl * hl, CI, 2 * W)
    sw = stride_weight.transpose(1, 0, 2).reshape(oc, 8 * CI)
    cot = cotangent.transpose(1, 0, 2, 3).reshape(dl, oc, H * W)
    wide = pltpu.VMEM((dl + 2, C, (hl + 2) * W), BF16)

    def sums(count, lanes):
        return [
            pltpu.VMEM((count, m, 2, hb, lanes), BF16),
            pltpu.VMEM((count, m, hb, lanes), BF16),
            pltpu.VMEM((count, m, hb, lanes), BF16),
            pltpu.VMEM((m - 1, count, hb, lanes), BF16),
            pltpu.VMEM((n // 2, count, hb, lanes), BF16),
        ]

    def sems(*shape):
        return [pltpu.SemaphoreType.DMA(shape)] * 2

    res, gs, gm, gl = pl.pallas_call(
        functools.partial(kernel, n, m, dl, hl, W),
        out_shape=(
            jax.ShapeDtypeStruct((dl, oc, H * W), BF16),
            jax.ShapeDtypeStruct((1, oc, 8 * CI), F32),
            jax.ShapeDtypeStruct((T, oc, C), F32),
            jax.ShapeDtypeStruct((T, oc, C), F32),
        ),
        in_specs=[pl.BlockSpec(memory_space=pltpu.VMEM)] * 5,
        out_specs=[pl.BlockSpec(memory_space=pltpu.VMEM)] * 4,
        scratch_shapes=[
            pltpu.VMEM((C, 8 * CI), BF16),
            pltpu.VMEM((T, C, C), BF16),
            pltpu.VMEM((T, C, C), BF16),
            wide, wide, wide, wide,
            pltpu.VMEM((8 * CI, dl * hl * W), BF16),
            pltpu.VMEM((dl, C, hl * W), F32),
            pltpu.VMEM((dl, C, hl * W), F32),
            pltpu.VMEM((dl, C, hl * W), BF16),
            *sums(1, 8 * CI),
            *sums(T, C),
            *sums(T, C),
            *sems(4, 8),
            *sems(3, m - 1),
            *sems(2, m - 1),
            *sems(2, m - 1),
            *sems(3),
            *sems(3, m - 1),
            *sems(3, n // 2 - 1),
            *sems(3),
        ],
        compiler_params=pltpu.CompilerParams(
            collective_id=0, has_side_effects=True, vmem_limit_bytes=52 * 1024 * 1024
        ),
    )(up, sw, middle_weight, last_weight, cot)
    result = res.reshape(dl, oc, H, W).transpose(1, 0, 2, 3)
    grad_stride = gs.reshape(oc, 8, CI).transpose(1, 0, 2)
    return (result, grad_stride, gm, gl)


def solution(mesh):
    weights = P(None, "filt", None)
    cells = P("filt", "depth", None, None)
    return jax.shard_map(
        functools.partial(per_device, mesh.shape["depth"], mesh.shape["filt"]),
        mesh=mesh,
        in_specs=(P(None, "depth", "filt", None), weights, weights, weights, cells),
        out_specs=(cells, weights, weights, weights),
        check_vma=False,
    )
```

profile of v0, /device:TPU:0, one launch (start us, length us, event | category | flops | bytes accessed | tf_op | source)
XLA Modules:
  0.0 80.8 jit_solution(7667983093087950693)
XLA Ops:
  0.6 0.0 copy-start.3
  0.6 0.0 copy-start.2
  0.7 0.9 %copy.10 = bf16[32,8,64]{2,1,0:T(8,128)(2,1)S(1)} copy(bf16[32,8,64]{2,0,1:T(8,128)(2,1)} %bitcast.27) | data formatting | bytes 65536 | tf_op jit(solution)/shard_map/transpose | solution.py:361
  1.6 0.1 reshape.24.sw
  1.7 0.0 copy-done.3
  1.8 0.0 copy-done.2
  1.8 0.0 copy-start
  1.8 0.0 copy-start.1
  1.8 1.0 %copy.9 = bf16[4,4,64,256]{3,2,1,0:T(8,128)(2,1)} copy(bf16[4,4,64,256]{3,1,0,2:T(4,128)(2,1)S(1)} %bitcast.23) | data formatting | bytes 1048576 | tf_op jit(solution)/shard_map/transpose | solution.py:360
  2.8 0.0 copy-done
  2.8 0.1 copy-done.1
  2.9 75.0 %shard_map.84 = (bf16[2,32,1024]{2,1,0:T(8,128)(2,1)S(1)}, f32[1,32,512]{2,1,0:T(8,128)S(1)}, f32[27,32,128]{2,1,0:T(8,128)S(1)}, f32[27,32,128]{2,1,0:T(8,128)S(1)}) custom-call(bf16[16,64,256]{2,1,0:T(8,128)(2,1)} %bitcast.22, bf16[32,512]{1,0:T(8,128)(2,1)S(1)} %reshape.24.sw, bf16[27,32,128]{2,1,0:T(8,128)(2,1)S(1)} %copy-done, ...), custom_call_target="tpu_custom_call" | custom-call | tf_op jit(solution)/shard_map/pallas_call | solution.py:377
  77.9 0.7 copy_bitcast_fusion.1
  78.6 0.1 reshape.27
  78.6 0.7 copy.18
  79.3 0.8 copy.21
  80.1 0.8 copy.22
  (3 shorter events, 0.1 us)
Async XLA Ops:
  0.6 1.1 %copy-start.3 = (bf16[32,2,8,128]{3,2,1,0:T(8,128)(2,1)S(1)}, bf16[32,2,8,128]{3,2,1,0:T(8,128)(2,1)}, u32[]{:S(2)}) copy-start(bf16[32,2,8,128]{3,2,1,0:T(8,128)(2,1)} %param.9) | copy-start | bytes 393220
  0.6 1.1 %copy-start.2 = (bf16[64,4,4,256]{3,2,1,0:T(4,128)(2,1)S(1)}, bf16[64,4,4,256]{3,2,1,0:T(4,128)(2,1)}, u32[]{:S(2)}) copy-start(bf16[64,4,4,256]{3,2,1,0:T(4,128)(2,1)} %param.5) | copy-start | bytes 1572868
  1.8 1.0 %copy-start = (bf16[27,32,128]{2,1,0:T(8,128)(2,1)S(1)}, bf16[27,32,128]{2,1,0:T(8,128)(2,1)}, u32[]{:S(2)}) copy-start(bf16[27,32,128]{2,1,0:T(8,128)(2,1)} %wm.1) | copy-start | bytes 663556
  1.8 1.1 %copy-start.1 = (bf16[27,32,128]{2,1,0:T(8,128)(2,1)S(1)}, bf16[27,32,128]{2,1,0:T(8,128)(2,1)}, u32[]{:S(2)}) copy-start(bf16[27,32,128]{2,1,0:T(8,128)(2,1)} %wl.1) | copy-start | bytes 663556
where the time goes:
time: 81.5 us; the launch traced here: 80.8 us
  Pallas kernels  75 us (92%)
  local copies, waits for them, and re-layouts  5.16 us (6%)
    pallas_call x1, Pallas kernels, per_device(): pl.pallas_call(functools.partial(kernel, n, m, dl, hl, W), out_shape=(jax...  75 us
    unnamed x11, local copies, waits for them, and re-layouts  1.65 us

commit v1 on v0

--- a/solution.py
+++ b/solution.py
@@ -31,23 +31,31 @@
     up, sw, wm, wl, cot,
     res, gs, gm, gl,
     SW, WM, WL, XL, XM, XG, XD, U, pre_l, pre_m, R,
-    pb_s, r1_s, z_s, zr_s, dr_s,
-    pb_m, r1_m, z_m, zr_m, dr_m,
-    pb_l, r1_l, z_l, zr_l, dr_l,
+    pb_s, r1_s, z_s, pr_s, y_s, zr_s,
+    pb_m, r1_m, z_m, pr_m, y_m, zr_m,
+    pb_l, r1_l, z_l, pr_l, y_l, zr_l,
     near_send, near_recv, swap_send, swap_recv,
-    wz_send, wz_recv, wp_send, wp_recv,
-    s1_send, s1_recv, s2_send, s2_recv, s3_send, s3_recv, s4_send, s4_recv,
+    wz_send, wz_recv, wg_send, wg_recv, wp_send, wp_recv,
+    s1_send, s1_recv, s2_send, s2_recv, s3_send, s3_recv, s4_send, s4_recv, s5_send, s5_recv,
 ):
     d, f = lax.axis_index("depth"), lax.axis_index("filt")
     oc, C = cot.shape[1], WM.shape[1]
     CI = up.shape[1]
     hb = oc // 2
-    half = lax.rem(d, 2)
+    T = wm.shape[0]
+    groups = n // 2
+    half, slot = lax.rem(d, 2), d // 2
     mate = d + 1 - 2 * half
     cols = hl * W
 
     for X in (XL, XM, XG, XD):
         X[...] = jnp.zeros_like(X)
+    for X, used in ((WM, T), (WL, T), (pb_m, T), (pb_l, T), (pb_s, 4)):
+        if X.shape[0] > used:
+            X[used:] = jnp.zeros((X.shape[0] - used,) + X.shape[1:], X.dtype)
+    own = pl.ds(pl.multiple_of(f * oc, oc), oc)
+    WM[:T, own, :] = wm[...]
+    WL[:T, own, :] = wl[...]
 
     def at(steps_d, steps_f):
         return (lax.rem(d + steps_d + n, n), lax.rem(f + steps_f + m, m))
@@ -67,7 +75,6 @@
     def mul(value, by):
         return pl.multiple_of(value * by, by)
 
-    own = pl.ds(mul(f, oc), oc)
     sends = []
     for k in range(1, m):
         where = at(0, k)
@@ -75,20 +82,21 @@
         copy.start()
         sends.append(copy)
 
-    def weight_out(index, src, dst):
+    def band(k):
+        return pl.ds(pl.multiple_of(lax.rem(f - k + m, m) * oc + half * hb, hb), hb)
+
+    def weight_out(index, dst):
         copies = []
-        part = pl.ds(mul(half, hb), hb)
-        spot = pl.ds(pl.multiple_of(f * oc + half * hb, hb), hb)
+        share = dst.shape[0] // groups
+        piece = dst.at[pl.ds(slot * share, share), band(0)]
         for k in range(1, m):
-            copy = remote(
-                src.at[:, part], dst.at[:, spot], wz_send.at[index, k - 1], wz_recv.at[index, k - 1], at(0, k)
-            )
+            copy = remote(piece, piece, wz_send.at[index, k - 1], wz_recv.at[index, k - 1], at(0, k))
             copy.start()
             copies.append(copy)
         return copies
 
     cot_copies = []
-    wm_copies = weight_out(0, wm, WM)
+    wm_copies = weight_out(0, WM)
     for k in range(1, m):
         where = at(0, k)
         copy = remote(
@@ -100,11 +108,9 @@
         )
         copy.start()
         cot_copies.append(copy)
-    wl_copies = weight_out(1, wl, WL)
+    wl_copies = weight_out(1, WL)
 
     SW[own, :] = sw[...]
-    WM[:, own, :] = wm[...]
-    WL[:, own, :] = wl[...]
     XG[pl.ds(1, dl), own, pl.ds(W, cols)] = cot[:, :, pl.ds(mul(f, cols), cols)]
 
     line = lax.broadcasted_iota(jnp.int32, (2 * W, 2 * W), 0)
@@ -203,7 +209,7 @@
         copy.start()
         return [copy]
 
-    def sum_2(index, copies, pb, r1, z, zr):
+    def sum_2(index, copies, pb, r1, z, pr):
         copies[0].wait()
 
         def body(t, carry):
@@ -211,69 +217,98 @@
             return carry
 
         lax.fori_loop(0, pb.shape[0], body, 0)
+        share = pb.shape[0] // groups
+        out = []
+        for j in range(1, groups):
+            where = at(2 * j, 0)
+            copy = remote(
+                z.at[pl.ds((where[0] // 2) * share, share)],
+                pr.at[j - 1],
+                s2_send.at[index, j - 1],
+                s2_recv.at[index, j - 1],
+                where,
+            )
+            copy.start()
+            out.append(copy)
+        return out
+
+    def sum_3(index, copies, z, pr, y, zr):
+        for copy in copies:
+            copy.wait()
+        share = y.shape[0]
+
+        def body(t, carry):
+            total = z[slot * share + t].astype(F32)
+            for j in range(groups - 1):
+                total += pr[j, t].astype(F32)
+            y[t] = total.astype(BF16)
+            return carry
+
+        lax.fori_loop(0, share, body, 0)
         out = []
         for k in range(1, m):
             where = at(0, k)
             copy = remote(
-                z.at[:, where[1]], zr.at[k - 1], s2_send.at[index, k - 1], s2_recv.at[index, k - 1], where
+                y.at[:, where[1]], zr.at[k - 1], s3_send.at[index, k - 1], s3_recv.at[index, k - 1], where
             )
             copy.start()
             out.append(copy)
         return out
 
-    def sum_3(index, copies, pb, r1, z, zr, dr):
+    def sum_4(index, copies, y, zr, out):
         for copy in copies:
             copy.wait()
-        slot = d // 2
+        share = y.shape[0]
+        part = pl.ds(mul(half, hb), hb)
 
         def body(t, carry):
-            total = pb[t, f, half].astype(F32) + r1[t, f].astype(F32)
+            total = y[t, f].astype(F32)
             for k in range(m - 1):
                 total += zr[k, t].astype(F32)
-            dr[slot, t] = total.astype(BF16)
+            out[slot * share + t, part, :] = total
             return carry
 
-        lax.fori_loop(0, pb.shape[0], body, 0)
+        lax.fori_loop(0, share, body, 0)
+        piece = out.at[pl.ds(slot * share, share), part]
+        copies = []
+        for j in range(1, groups):
+            copy = remote(piece, piece, s4_send.at[index, j - 1], s4_recv.at[index, j - 1], at(2 * j, 0))
+            copy.start()
+            copies.append(copy)
+        return copies
+
+    def sum_5(index, copies, out):
+        for copy in copies:
+            copy.wait()
+        part = pl.ds(mul(half, hb), hb)
+        copy = remote(out.at[:, part], out.at[:, part], s5_send.at[index], s5_recv.at[index], (mate, f))
+        copy.start()
+        return [copy]
+
+    def weight_spread(index, copies, dst):
+        share = dst.shape[0] // groups
         out = []
-        for j in range(1, n // 2):
-            copy = remote(
-                dr.at[slot], dr.at[slot], s3_send.at[index, j - 1], s3_recv.at[index, j - 1], at(2 * j, 0)
-            )
+        for k in range(1, m):
+            copies[k - 1].wait()
+            piece = dst.at[pl.ds(slot * share, share), band(k)]
+            for j in range(1, groups):
+                copy = remote(
+                    piece, piece, wg_send.at[index, k - 1, j - 1], wg_recv.at[index, k - 1, j - 1], at(2 * j, 0)
+                )
+                copy.start()
+                out.append(copy)
+        return out
+
+    def weight_pass(index, copies, dst):
+        out = []
+        for k in range(1, m):
+            for copy in copies[(k - 1) * (groups - 1) : k * (groups - 1)]:
+                copy.wait()
+            piece = dst.at[:, band(k)]
+            copy = remote(piece, piece, wp_send.at[index, k - 1], wp_recv.at[index, k - 1], (mate, f))
             copy.start()
             out.append(copy)
         return out
-
-    def sum_4(index, copies, dr, out):
-        for copy in copies:
-            copy.wait()
-        part = pl.ds(mul(half, hb), hb)
-
-        def body(t, carry):
-            total = dr[0, t].astype(F32)
-            for j in range(1, n // 2):
-                total += dr[j, t].astype(F32)
-            out[t, part, :] = total
-            return carry
-
-        lax.fori_loop(0, out.shape[0], body, 0)
-        copy = remote(out.at[:, part], out.at[:, part], s4_send.at[index], s4_recv.at[index], (mate, f))
-        copy.start()
-        return [copy]
-
-    def weight_pass(index, copies, dst):
-        out = []
-        for k in range(1, m):
-            copies[k - 1].wait()
-            spot = pl.ds(pl.multiple_of(lax.rem(f - k + m, m) * oc + half * hb, hb), hb)
-            copy = remote(
-                dst.at[:, spot], dst.at[:, spot], wp_send.at[index, k - 1], wp_recv.at[index, k - 1], (mate, f)
-            )
-            copy.start()
-            out.append(copy)
-        return out
-
-    def flat(X, plane):
-        return X[plane + 1, :, W : W + cols]
 
     for copy in sends:
         copy.wait()
@@ -282,10 +317,12 @@
         pre_l[plane] = value
         XL[plane + 1, :, W : W + cols] = silu(value).astype(BF16)
     near_start(0, XL)
-    wm_pass = weight_pass(0, wm_copies, WM)
+    wm_pass = weight_spread(0, wm_copies, WM)
     for copy in cot_copies:
         copy.wait()
     near_start(1, XG)
+    wm_pass = weight_pass(0, wm_pass, WM)
+    wl_pass = weight_spread(1, wl_copies, WL)
     near_wait(0, XL)
     for copy in wm_pass:
         copy.wait()
@@ -294,7 +331,7 @@
         pre_m[plane] = value
         XM[plane + 1, :, W : W + cols] = silu(value).astype(BF16)
     near_start(2, XM)
-    wl_pass = weight_pass(1, wl_copies, WL)
+    wl_pass = weight_pass(1, wl_pass, WL)
     near_wait(1, XG)
     for copy in wl_pass:
         copy.wait()
@@ -303,12 +340,12 @@
         value = conv_back(XG, WL, plane) * silu_slope(pre_m[plane])
         XD[plane + 1, :, W : W + cols] = value.astype(BF16)
     near_start(3, XD)
-    weight_grad(XD, XL, pb_m)
-    sum_m = sum_1(0, pb_m, r1_m)
     near_wait(2, XM)
     weight_grad(XG, XM, pb_l)
     sum_l = sum_1(1, pb_l, r1_l)
-    sum_m = sum_2(0, sum_m, pb_m, r1_m, z_m, zr_m)
+    weight_grad(XD, XL, pb_m)
+    sum_m = sum_1(0, pb_m, r1_m)
+    sum_l = sum_2(1, sum_l, pb_l, r1_l, z_l, pr_l)
     near_wait(3, XD)
     left = []
     for plane in range(dl):
@@ -317,10 +354,13 @@
     total = dot(left[0], U[:, :cols], (1, 1))
     for plane in range(1, dl):
         total += dot(left[plane], U[:, plane * cols : (plane + 1) * cols], (1, 1))
-    pb_s[...] = total.astype(BF16).reshape(pb_s.shape)
+    total = total.astype(BF16)
+    for pair in range(4):
+        pb_s[pair] = total[:, pair * 2 * CI : (pair + 1) * 2 * CI].reshape(pb_s.shape[1:])
     sum_s = sum_1(2, pb_s, r1_s)
-    sum_l = sum_2(1, sum_l, pb_l, r1_l, z_l, zr_l)
-    sum_s = sum_2(2, sum_s, pb_s, r1_s, z_s, zr_s)
+    sum_m = sum_2(0, sum_m, pb_m, r1_m, z_m, pr_m)
+    sum_s = sum_2(2, sum_s, pb_s, r1_s, z_s, pr_s)
+    sum_l = sum_3(1, sum_l, z_l, pr_l, y_l, zr_l)
 
     for plane in range(dl):
         R[plane] = conv(XM, WL, plane).astype(BF16)
@@ -339,12 +379,14 @@
         out_copies.append(copy)
     res[:, :, out_spot] = R[:, own]
 
-    sum_m = sum_3(0, sum_m, pb_m, r1_m, z_m, zr_m, dr_m)
-    sum_l = sum_3(1, sum_l, pb_l, r1_l, z_l, zr_l, dr_l)
-    sum_s = sum_3(2, sum_s, pb_s, r1_s, z_s, zr_s, dr_s)
-    sum_m = sum_4(0, sum_m, dr_m, gm)
-    sum_l = sum_4(1, sum_l, dr_l, gl)
-    sum_s = sum_4(2, sum_s, dr_s, gs)
+    sum_m = sum_3(0, sum_m, z_m, pr_m, y_m, zr_m)
+    sum_s = sum_3(2, sum_s, z_s, pr_s, y_s, zr_s)
+    sum_l = sum_4(1, sum_l, y_l, zr_l, gl)
+    sum_m = sum_4(0, sum_m, y_m, zr_m, gm)
+    sum_s = sum_4(2, sum_s, y_s, zr_s, gs)
+    sum_l = sum_5(1, sum_l, gl)
+    sum_m = sum_5(0, sum_m, gm)
+    sum_s = sum_5(2, sum_s, gs)
     for copy in out_copies + sum_m + sum_l + sum_s:
         copy.wait()
     for index, X in enumerate((XL, XG, XM, XD)):
@@ -362,13 +404,18 @@
     cot = cotangent.transpose(1, 0, 2, 3).reshape(dl, oc, H * W)
     wide = pltpu.VMEM((dl + 2, C, (hl + 2) * W), BF16)
 
+    groups = n // 2
+    TP, SP = -(-T // groups) * groups, -(-4 // groups) * groups
+
     def sums(count, lanes):
+        share = count // groups
         return [
             pltpu.VMEM((count, m, 2, hb, lanes), BF16),
             pltpu.VMEM((count, m, hb, lanes), BF16),
             pltpu.VMEM((count, m, hb, lanes), BF16),
-            pltpu.VMEM((m - 1, count, hb, lanes), BF16),
-            pltpu.VMEM((n // 2, count, hb, lanes), BF16),
+            pltpu.VMEM((groups - 1, share, m, hb, lanes), BF16),
+            pltpu.VMEM((share, m, hb, lanes), BF16),
+            pltpu.VMEM((m - 1, share, hb, lanes), BF16),
         ]
 
     def sems(*shape):
@@ -378,31 +425,33 @@
         functools.partial(kernel, n, m, dl, hl, W),
         out_shape=(
             jax.ShapeDtypeStruct((dl, oc, H * W), BF16),
-            jax.ShapeDtypeStruct((1, oc, 8 * CI), F32),
-            jax.ShapeDtypeStruct((T, oc, C), F32),
-            jax.ShapeDtypeStruct((T, oc, C), F32),
+            jax.ShapeDtypeStruct((SP, oc, 2 * CI), F32),
+            jax.ShapeDtypeStruct((TP, oc, C), F32),
+            jax.ShapeDtypeStruct((TP, oc, C), F32),
         ),
         in_specs=[pl.BlockSpec(memory_space=pltpu.VMEM)] * 5,
         out_specs=[pl.BlockSpec(memory_space=pltpu.VMEM)] * 4,
         scratch_shapes=[
             pltpu.VMEM((C, 8 * CI), BF16),
-            pltpu.VMEM((T, C, C), BF16),
-            pltpu.VMEM((T, C, C), BF16),
+            pltpu.VMEM((TP, C, C), BF16),
+            pltpu.VMEM((TP, C, C), BF16),
             wide, wide, wide, wide,
             pltpu.VMEM((8 * CI, dl * hl * W), BF16),
             pltpu.VMEM((dl, C, hl * W), F32),
             pltpu.VMEM((dl, C, hl * W), F32),
             pltpu.VMEM((dl, C, hl * W), BF16),
-            *sums(1, 8 * CI),
-            *sums(T, C),
-            *sums(T, C),
+            *sums(SP, 2 * CI),
+            *sums(TP, C),
+            *sums(TP, C),
             *sems(4, 8),
             *sems(3, m - 1),
             *sems(2, m - 1),
+            *sems(2, m - 1, groups - 1),
             *sems(2, m - 1),
             *sems(3),
+            *sems(3, groups - 1),
             *sems(3, m - 1),
-            *sems(3, n // 2 - 1),
+            *sems(3, groups - 1),
             *sems(3),
         ],
         compiler_params=pltpu.CompilerParams(
@@ -410,8 +459,8 @@
         ),
     )(up, sw, middle_weight, last_weight, cot)
     result = res.reshape(dl, oc, H, W).transpose(1, 0, 2, 3)
-    grad_stride = gs.reshape(oc, 8, CI).transpose(1, 0, 2)
-    return (result, grad_stride, gm, gl)
+    grad_stride = gs[:4].reshape(4, oc, 2, CI).transpose(0, 2, 1, 3).reshape(8, oc, CI)
+    return (result, grad_stride, gm[:T], gl[:T])
 
 
 def solution(mesh):

time: 81.5 us -> 65.3 us (0.80)
  Pallas kernels: 75 us -> 59.2 us
    pallas_call x1, Pallas kernels: 75 us -> 59.2 us  [per_device(): pl.pallas_call(functools.partial(kernel, n, m, dl, hl, W), out_shape=(jax...]
    slice x0 -> x3, local copies, waits for them, and re-layouts: none -> 1.66 us  [the longest x2 1.58 us: per_device(): return (result, grad_stride, gm[:T], gl[:T])]
    unnamed x11 -> x9, local copies, waits for them, and re-layouts: 1.65 us -> 0.14 us
where the time goes in v1:
time: 65.3 us; the launch traced here: 65.1 us
  Pallas kernels  59.2 us (91%)
  local copies, waits for them, and re-layouts  4.53 us (7%)
  between operations  0.71 us (1%)
  other arithmetic  0.67 us (1%)
    pallas_call x1, Pallas kernels, per_device(): pl.pallas_call(functools.partial(kernel, n, m, dl, hl, W), out_shape=(jax...  59.2 us
    slice x2, local copies, waits for them, and re-layouts, per_device(): return (result, grad_stride, gm[:T], gl[:T])  1.58 us

profile of v1, /device:TPU:0, one launch (start us, length us, event | category | flops | bytes accessed | tf_op | source)
XLA Modules:
  0.0 65.1 jit_solution(9657681619216395686)
XLA Ops:
  0.6 0.0 copy-start.3
  0.6 0.0 copy-start.2
  0.7 0.9 %copy.10 = bf16[32,8,64]{2,1,0:T(8,128)(2,1)S(1)} copy(bf16[32,8,64]{2,0,1:T(8,128)(2,1)} %bitcast.25) | data formatting | bytes 65536 | tf_op jit(solution)/shard_map/transpose | solution.py:403
  1.6 0.1 reshape.25.sw
  1.7 0.0 copy-done.3
  1.8 0.0 copy-done.2
  1.8 0.0 copy-start
  1.8 0.0 copy-start.1
  1.8 0.9 %copy.9 = bf16[4,4,64,256]{3,2,1,0:T(8,128)(2,1)} copy(bf16[4,4,64,256]{3,1,0,2:T(4,128)(2,1)S(1)} %bitcast.21) | data formatting | bytes 1048576 | tf_op jit(solution)/shard_map/transpose | solution.py:402
  2.8 0.0 copy-done
  2.8 0.1 copy-done.1
  2.9 59.2 %shard_map.84 = (bf16[2,32,1024]{2,1,0:T(8,128)(2,1)S(1)}, f32[4,32,128]{2,1,0:T(8,128)S(1)}, f32[28,32,128]{2,1,0:T(8,128)S(1)}, f32[28,32,128]{2,1,0:T(8,128)S(1)}) custom-call(bf16[16,64,256]{2,1,0:T(8,128)(2,1)} %bitcast.20, bf16[32,512]{1,0:T(8,128)(2,1)S(1)} %reshape.25.sw, bf16[27,32,128]{2,1,0:T(8,128)(2,1)S(1)} %copy-done, ...), custom_call_target="tpu_custom_call" | custom-call | tf_op jit(solution)/shard_map/pallas_call | solution.py:424
  62.1 0.7 %copy_bitcast_fusion = bf16[32,2,8,128]{3,2,1,0:T(8,128)(2,1)} fusion(bf16[2,32,8,128]{3,2,1,0:T(8,128)(2,1)S(1)} %bitcast.22), kind=kLoop, calls=%fused_computation.1 | loop fusion | bytes 262144 | tf_op jit(solution)/shard_map/transpose | solution.py:461
  62.8 0.1 fusion
  62.8 0.7 %pad_maximum_fusion = f32[4,64,64]{2,1,0:T(8,128)} fusion(f32[4,32,64]{2,1,0:T(8,128)S(1)} %get-tuple-element.13, f32[4,32,64]{2,1,0:T(8,128)S(1)} %get-tuple-element.12), kind=kLoop, calls=%fused_computation | loop fusion | flops 16384 | bytes 131072 | tf_op jit(solution)/shard_map/concatenate
  63.5 0.8 %slice.14 = f32[27,32,128]{2,1,0:T(8,128)} slice(f32[28,32,128]{2,1,0:T(8,128)S(1)} %get-tuple-element.10), slice={[0:27], [0:32], [0:128]} | slice | bytes 884736 | tf_op jit(solution)/shard_map/slice | solution.py:463
  64.3 0.8 %slice.15 = f32[27,32,128]{2,1,0:T(8,128)} slice(f32[28,32,128]{2,1,0:T(8,128)S(1)} %get-tuple-element.11), slice={[0:27], [0:32], [0:128]} | slice | bytes 884736 | tf_op jit(solution)/shard_map/slice | solution.py:463
  (3 shorter events, 0.1 us)
Async XLA Ops:
  0.6 1.1 %copy-start.3 = (bf16[32,2,8,128]{3,2,1,0:T(8,128)(2,1)S(1)}, bf16[32,2,8,128]{3,2,1,0:T(8,128)(2,1)}, u32[]{:S(2)}) copy-start(bf16[32,2,8,128]{3,2,1,0:T(8,128)(2,1)} %param.9) | copy-start | bytes 393220
  0.6 1.1 %copy-start.2 = (bf16[64,4,4,256]{3,2,1,0:T(4,128)(2,1)S(1)}, bf16[64,4,4,256]{3,2,1,0:T(4,128)(2,1)}, u32[]{:S(2)}) copy-start(bf16[64,4,4,256]{3,2,1,0:T(4,128)(2,1)} %param.5) | copy-start | bytes 1572868
  1.8 1.0 %copy-start = (bf16[27,32,128]{2,1,0:T(8,128)(2,1)S(1)}, bf16[27,32,128]{2,1,0:T(8,128)(2,1)}, u32[]{:S(2)}) copy-start(bf16[27,32,128]{2,1,0:T(8,128)(2,1)} %wm.1) | copy-start | bytes 663556
  1.8 1.1 %copy-start.1 = (bf16[27,32,128]{2,1,0:T(8,128)(2,1)S(1)}, bf16[27,32,128]{2,1,0:T(8,128)(2,1)}, u32[]{:S(2)}) copy-start(bf16[27,32,128]{2,1,0:T(8,128)(2,1)} %wl.1) | copy-start | bytes 663556

commit v2 on v1

--- a/solution.py
+++ b/solution.py
@@ -10,6 +10,7 @@
 F32 = jnp.float32
 BF16 = jnp.bfloat16
 MESH = pl.DeviceIdType.MESH
+CHUNKS = (15, 12, 15, 12, 4)
 NEAR = [(z, y) for z in (-1, 0, 1) for y in (-1, 0, 1) if (z, y) != (0, 0)]
 
 
@@ -29,15 +30,16 @@
 def kernel(
     n, m, dl, hl, W,
     up, sw, wm, wl, cot,
-    res, gs, gm, gl,
-    SW, WM, WL, XL, XM, XG, XD, U, pre_l, pre_m, R,
-    pb_s, r1_s, z_s, pr_s, y_s, zr_s,
-    pb_m, r1_m, z_m, pr_m, y_m, zr_m,
-    pb_l, r1_l, z_l, pr_l, y_l, zr_l,
+    *refs,
+):
+    res, *outs = refs[:6]
+    SW, WM, WL, XL, XM, XG, XD, U, pre_l, pre_m, R = refs[6:17]
+    bufs = [refs[17 + 6 * i : 23 + 6 * i] for i in range(5)]
+    (
     near_send, near_recv, swap_send, swap_recv,
     wz_send, wz_recv, wg_send, wg_recv, wp_send, wp_recv,
     s1_send, s1_recv, s2_send, s2_recv, s3_send, s3_recv, s4_send, s4_recv, s5_send, s5_recv,
-):
+    ) = refs[47:]
     d, f = lax.axis_index("depth"), lax.axis_index("filt")
     oc, C = cot.shape[1], WM.shape[1]
     CI = up.shape[1]
@@ -50,12 +52,14 @@
 
     for X in (XL, XM, XG, XD):
         X[...] = jnp.zeros_like(X)
-    for X, used in ((WM, T), (WL, T), (pb_m, T), (pb_l, T), (pb_s, 4)):
+    for X, used in ((WM, T), (WL, T), *((bufs[i][0], CHUNKS[i]) for i in range(5))):
         if X.shape[0] > used:
             X[used:] = jnp.zeros((X.shape[0] - used,) + X.shape[1:], X.dtype)
     own = pl.ds(pl.multiple_of(f * oc, oc), oc)
     WM[:T, own, :] = wm[...]
     WL[:T, own, :] = wl[...]
+    for tap in range(8):
+        SW[own, tap * CI : (tap + 1) * CI] = sw[tap]
 
     def at(steps_d, steps_f):
         return (lax.rem(d + steps_d + n, n), lax.rem(f + steps_f + m, m))
@@ -78,7 +82,7 @@
     sends = []
     for k in range(1, m):
         where = at(0, k)
-        copy = remote(sw, SW.at[own], swap_send.at[0, k - 1], swap_recv.at[0, k - 1], where)
+        copy = remote(SW.at[own], SW.at[own], swap_send.at[0, k - 1], swap_recv.at[0, k - 1], where)
         copy.start()
         sends.append(copy)
 
@@ -95,22 +99,7 @@
             copies.append(copy)
         return copies
 
-    cot_copies = []
     wm_copies = weight_out(0, WM)
-    for k in range(1, m):
-        where = at(0, k)
-        copy = remote(
-            cot.at[:, :, pl.ds(mul(where[1], cols), cols)],
-            XG.at[pl.ds(1, dl), own, pl.ds(W, cols)],
-            swap_send.at[1, k - 1],
-            swap_recv.at[1, k - 1],
-            where,
-        )
-        copy.start()
-        cot_copies.append(copy)
-    wl_copies = weight_out(1, WL)
-
-    SW[own, :] = sw[...]
     XG[pl.ds(1, dl), own, pl.ds(W, cols)] = cot[:, :, pl.ds(mul(f, cols), cols)]
 
     line = lax.broadcasted_iota(jnp.int32, (2 * W, 2 * W), 0)
@@ -190,19 +179,21 @@
             parts.append(total)
         return after(parts[0]) + parts[1] + before(parts[2])
 
-    def weight_grad(D, X, out):
+    def grad_left(D):
         left = []
         for plane in range(dl):
             value = D[plane + 1, :, W : W + cols]
             wide = value.astype(F32)
             left.append(jnp.concatenate([after(wide).astype(BF16), value, before(wide).astype(BF16)], axis=0))
-        for a in range(3):
-            for b in range(3):
-                total = dot(left[0], X[a, :, b * W : b * W + cols], (1, 1))
-                for plane in range(1, dl):
-                    total += dot(left[plane], X[plane + a, :, b * W : b * W + cols], (1, 1))
-                tap = 9 * a + 3 * b
-                out[tap : tap + 3] = total.astype(BF16).reshape(3, m, 2, hb, C)
+        return left
+
+    def weight_grad(left, X, out, lines):
+        for number, line in enumerate(lines):
+            a, b = line // 3, line % 3
+            total = dot(left[0], X[a, :, b * W : b * W + cols], (1, 1))
+            for plane in range(1, dl):
+                total += dot(left[plane], X[plane + a, :, b * W : b * W + cols], (1, 1))
+            out[3 * number : 3 * number + 3] = total.astype(BF16).reshape(3, m, 2, hb, C)
 
     def sum_1(index, pb, r1):
         copy = remote(pb.at[:, :, 1 - half], r1, s1_send.at[index], s1_recv.at[index], (mate, f))
@@ -265,7 +256,7 @@
             total = y[t, f].astype(F32)
             for k in range(m - 1):
                 total += zr[k, t].astype(F32)
-            out[slot * share + t, part, :] = total
+            out[slot * share + t, part, :] = total.astype(BF16)
             return carry
 
         lax.fori_loop(0, share, body, 0)
@@ -317,12 +308,25 @@
         pre_l[plane] = value
         XL[plane + 1, :, W : W + cols] = silu(value).astype(BF16)
     near_start(0, XL)
+    wl_copies = weight_out(1, WL)
+    cot_copies = []
+    for k in range(1, m):
+        where = at(0, k)
+        copy = remote(
+            cot.at[:, :, pl.ds(mul(where[1], cols), cols)],
+            XG.at[pl.ds(1, dl), own, pl.ds(W, cols)],
+            swap_send.at[1, k - 1],
+            swap_recv.at[1, k - 1],
+            where,
+        )
+        copy.start()
+        cot_copies.append(copy)
     wm_pass = weight_spread(0, wm_copies, WM)
+    wm_pass = weight_pass(0, wm_pass, WM)
+    wl_pass = weight_spread(1, wl_copies, WL)
     for copy in cot_copies:
         copy.wait()
     near_start(1, XG)
-    wm_pass = weight_pass(0, wm_pass, WM)
-    wl_pass = weight_spread(1, wl_copies, WL)
     near_wait(0, XL)
     for copy in wm_pass:
         copy.wait()
@@ -341,11 +345,33 @@
         XD[plane + 1, :, W : W + cols] = value.astype(BF16)
     near_start(3, XD)
     near_wait(2, XM)
-    weight_grad(XG, XM, pb_l)
-    sum_l = sum_1(1, pb_l, r1_l)
-    weight_grad(XD, XL, pb_m)
-    sum_m = sum_1(0, pb_m, r1_m)
-    sum_l = sum_2(1, sum_l, pb_l, r1_l, z_l, pr_l)
+    going = {}
+
+    def step(number, index):
+        pb, r1, z, pr, y, zr = bufs[index]
+        if number == 1:
+            going[index] = sum_1(index, pb, r1)
+        elif number == 2:
+            going[index] = sum_2(index, going[index], pb, r1, z, pr)
+        elif number == 3:
+            going[index] = sum_3(index, going[index], z, pr, y, zr)
+        elif number == 4:
+            going[index] = sum_4(index, going[index], y, zr, outs[index])
+        else:
+            going[index] = sum_5(index, going[index], outs[index])
+
+    left = grad_left(XG)
+    weight_grad(left, XM, bufs[0][0], range(5))
+    step(1, 0)
+    weight_grad(left, XM, bufs[1][0], range(5, 9))
+    step(1, 1)
+    left = grad_left(XD)
+    weight_grad(left, XL, bufs[2][0], range(5))
+    step(1, 2)
+    step(2, 0)
+    weight_grad(left, XL, bufs[3][0], range(5, 9))
+    step(1, 3)
+    step(2, 1)
     near_wait(3, XD)
     left = []
     for plane in range(dl):
@@ -356,11 +382,10 @@
         total += dot(left[plane], U[:, plane * cols : (plane + 1) * cols], (1, 1))
     total = total.astype(BF16)
     for pair in range(4):
-        pb_s[pair] = total[:, pair * 2 * CI : (pair + 1) * 2 * CI].reshape(pb_s.shape[1:])
-    sum_s = sum_1(2, pb_s, r1_s)
-    sum_m = sum_2(0, sum_m, pb_m, r1_m, z_m, pr_m)
-    sum_s = sum_2(2, sum_s, pb_s, r1_s, z_s, pr_s)
-    sum_l = sum_3(1, sum_l, z_l, pr_l, y_l, zr_l)
+        bufs[4][0][pair] = total[:, pair * 2 * CI : (pair + 1) * 2 * CI].reshape(bufs[4][0].shape[1:])
+    step(1, 4)
+    for number, index in ((2, 2), (2, 3), (2, 4), (3, 0), (3, 1)):
+        step(number, index)
 
     for plane in range(dl):
         R[plane] = conv(XM, WL, plane).astype(BF16)
@@ -379,15 +404,11 @@
         out_copies.append(copy)
     res[:, :, out_spot] = R[:, own]
 
-    sum_m = sum_3(0, sum_m, z_m, pr_m, y_m, zr_m)
-    sum_s = sum_3(2, sum_s, z_s, pr_s, y_s, zr_s)
-    sum_l = sum_4(1, sum_l, y_l, zr_l, gl)
-    sum_m = sum_4(0, sum_m, y_m, zr_m, gm)
-    sum_s = sum_4(2, sum_s, y_s, zr_s, gs)
-    sum_l = sum_5(1, sum_l, gl)
-    sum_m = sum_5(0, sum_m, gm)
-    sum_s = sum_5(2, sum_s, gs)
-    for copy in out_copies + sum_m + sum_l + sum_s:
+    for number, index in (
+        (3, 2), (4, 0), (3, 3), (4, 1), (3, 4), (5, 0), (4, 2), (5, 1), (4, 3), (4, 4), (5, 2), (5, 3), (5, 4)
+    ):
+        step(number, index)
+    for copy in out_copies + [copy for copies in going.values() for copy in copies]:
         copy.wait()
     for index, X in enumerate((XL, XG, XM, XD)):
         near_end(index, X)
@@ -400,12 +421,13 @@
     T = middle_weight.shape[0]
     hb = oc // 2
     up = upper_level.transpose(1, 2, 0, 3).reshape(4 * dl * hl, CI, 2 * W)
-    sw = stride_weight.transpose(1, 0, 2).reshape(oc, 8 * CI)
     cot = cotangent.transpose(1, 0, 2, 3).reshape(dl, oc, H * W)
     wide = pltpu.VMEM((dl + 2, C, (hl + 2) * W), BF16)
 
     groups = n // 2
-    TP, SP = -(-T // groups) * groups, -(-4 // groups) * groups
+    TP = -(-T // groups) * groups
+    sizes = [-(-count // groups) * groups for count in CHUNKS]
+    lanes = [C] * 4 + [2 * CI]
 
     def sums(count, lanes):
         share = count // groups
@@ -421,16 +443,14 @@
     def sems(*shape):
         return [pltpu.SemaphoreType.DMA(shape)] * 2
 
-    res, gs, gm, gl = pl.pallas_call(
+    res, *grads = pl.pallas_call(
         functools.partial(kernel, n, m, dl, hl, W),
         out_shape=(
             jax.ShapeDtypeStruct((dl, oc, H * W), BF16),
-            jax.ShapeDtypeStruct((SP, oc, 2 * CI), F32),
-            jax.ShapeDtypeStruct((TP, oc, C), F32),
-            jax.ShapeDtypeStruct((TP, oc, C), F32),
+            *(jax.ShapeDtypeStruct((size, oc, wide_), BF16) for size, wide_ in zip(sizes, lanes)),
         ),
         in_specs=[pl.BlockSpec(memory_space=pltpu.VMEM)] * 5,
-        out_specs=[pl.BlockSpec(memory_space=pltpu.VMEM)] * 4,
+        out_specs=[pl.BlockSpec(memory_space=pltpu.VMEM)] * 6,
         scratch_shapes=[
             pltpu.VMEM((C, 8 * CI), BF16),
             pltpu.VMEM((TP, C, C), BF16),
@@ -440,27 +460,45 @@
             pltpu.VMEM((dl, C, hl * W), F32),
             pltpu.VMEM((dl, C, hl * W), F32),
             pltpu.VMEM((dl, C, hl * W), BF16),
-            *sums(SP, 2 * CI),
-            *sums(TP, C),
-            *sums(TP, C),
+            *(buf for size, wide_ in zip(sizes, lanes) for buf in sums(size, wide_)),
             *sems(4, 8),
             *sems(3, m - 1),
             *sems(2, m - 1),
             *sems(2, m - 1, groups - 1),
             *sems(2, m - 1),
-            *sems(3),
-            *sems(3, groups - 1),
-            *sems(3, m - 1),
-            *sems(3, groups - 1),
-            *sems(3),
+            *sems(5),
+            *sems(5, groups - 1),
+            *sems(5, m - 1),
+            *sems(5, groups - 1),
+            *sems(5),
         ],
         compiler_params=pltpu.CompilerParams(
             collective_id=0, has_side_effects=True, vmem_limit_bytes=52 * 1024 * 1024
         ),
-    )(up, sw, middle_weight, last_weight, cot)
+    )(up, stride_weight, middle_weight, last_weight, cot)
     result = res.reshape(dl, oc, H, W).transpose(1, 0, 2, 3)
-    grad_stride = gs[:4].reshape(4, oc, 2, CI).transpose(0, 2, 1, 3).reshape(8, oc, CI)
-    return (result, grad_stride, gm[:T], gl[:T])
+    gs, gm, gl = pl.pallas_call(
+        widen,
+        out_shape=(
+            jax.ShapeDtypeStruct((8, oc, CI), F32),
+            jax.ShapeDtypeStruct((T, oc, C), F32),
+            jax.ShapeDtypeStruct((T, oc, C), F32),
+        ),
+    )(*grads)
+    return (result, gs, gm, gl)
+
+
+def widen(last_0, last_1, middle_0, middle_1, stride, gs, gm, gl):
+    for source, target, start, count in (
+        (last_0, gl, 0, CHUNKS[0]),
+        (last_1, gl, CHUNKS[0], CHUNKS[1]),
+        (middle_0, gm, 0, CHUNKS[2]),
+        (middle_1, gm, CHUNKS[2], CHUNKS[3]),
+    ):
+        target[start : start + count] = source[:count].astype(F32)
+    CI = gs.shape[2]
+    for tap in range(8):
+        gs[tap] = stride[tap // 2].astype(F32)[:, (tap % 2) * CI : (tap % 2 + 1) * CI]
 
 
 def solution(mesh):

time: 65.3 us -> 65.5 us (level)
  local copies, waits for them, and re-layouts: 4.53 us -> 5.39 us
  other arithmetic: 0.67 us -> 0 us
    unnamed x9 -> x19, local copies, waits for them, and re-layouts: 0.14 us -> 3.53 us
    pallas_call x0 -> x1, Pallas kernels: none -> 2.04 us  [per_device(): pl.pallas_call(widen, out_shape=(jax.ShapeDtypeStruct((8, oc, CI), F32),...]
    pallas_call x1, Pallas kernels: 59.2 us -> 57.3 us  [per_device(): pl.pallas_call(functools.partial(kernel, n, m, dl, hl, W), out_shape=(jax...]
    slice x3 -> x0, local copies, waits for them, and re-layouts: 1.66 us -> none  [the longest x2 1.58 us: per_device(): return (result, grad_stride, gm[:T], gl[:T])]
    reshape x2, local copies, waits for them, and re-layouts: 0.06 us -> 1.02 us  [per_device(): cot = cotangent.transpose(1, 0, 2, 3).reshape(dl, oc, H * W)]
    transpose x1 -> x0, local copies, waits for them, and re-layouts: 0.93 us -> none  [per_device(): sw = stride_weight.transpose(1, 0, 2).reshape(oc, 8 * CI)]
    transpose x1, local copies, waits for them, and re-layouts: 0.95 us -> 0.16 us  [per_device(): up = upper_level.transpose(1, 2, 0, 3).reshape(4 * dl * hl, CI, 2 * W)]
    concatenate x1 -> x0, other arithmetic: 0.67 us -> none
where the time goes in v2:
time: 65.5 us; the launch traced here: 65.4 us
  Pallas kernels  59.3 us (91%)
  local copies, waits for them, and re-layouts  5.39 us (8%)
  between operations  0.68 us (1%)
    pallas_call x1, Pallas kernels, per_device(): pl.pallas_call(functools.partial(kernel, n, m, dl, hl, W), out_shape=(jax...  57.3 us
    unnamed x19, local copies, waits for them, and re-layouts  3.53 us
    pallas_call x1, Pallas kernels, per_device(): pl.pallas_call(widen, out_shape=(jax.ShapeDtypeStruct((8, oc, CI), F32),...  2.04 us

profile of v2, /device:TPU:0, one launch (start us, length us, event | category | flops | bytes accessed | tf_op | source)
XLA Modules:
  0.0 65.4 jit_solution(17401413846561671934)
XLA Ops:
  0.6 0.0 copy-start.8
  0.6 1.0 %reshape.20 = bf16[2,32,1024]{2,0,1:T(2,128)(2,1)S(1)} reshape(bf16[2,32,8,128]{3,2,0,1:T(8,128)(2,1)} %bitcast.21) | data formatting | bytes 262144 | tf_op jit(solution)/shard_map/reshape | solution.py:424
  1.7 0.1 copy-done.8
  1.7 0.0 copy-start
  1.7 0.0 copy-start.1
  1.7 0.0 copy-start.6
  1.7 0.2 copy.9
  1.9 0.8 %copy-done = bf16[27,32,128]{2,1,0:T(8,128)(2,1)S(1)} copy-done((bf16[27,32,128]{2,1,0:T(8,128)(2,1)S(1)}, bf16[27,32,128]{2,1,0:T(8,128)(2,1)}, u32[]{:S(2)}) %copy-start) | copy-done | bytes 221208
  2.7 0.1 copy-done.1
  2.8 0.0 copy-done.6
  2.8 57.3 %shard_map.84 = (bf16[2,32,1024]{2,1,0:T(8,128)(2,1)S(1)}, bf16[16,32,128]{2,1,0:T(8,128)(2,1)S(1)}, bf16[12,32,128]{2,1,0:T(8,128)(2,1)S(1)}, bf16[16,32,128]{2...) custom-call(bf16[16,64,256]{2,1,0:T(8,128)(2,1)S(1)} %bitcast.17, ...), custom_call_target="tpu_custom_call" | custom-call | tf_op jit(solution)/shard_map/pallas_call | solution.py:446
  60.1 0.0 copy-start.4
  60.1 0.6 copy-done.4
  60.7 0.0 copy-start.5
  60.7 0.6 copy-done.5
  61.3 0.0 copy-start.7
  61.3 0.6 copy-done.7
  61.9 0.0 copy-start.2
  61.9 0.0 copy-start.3
  62.0 0.6 copy-done.2
  62.6 0.1 copy-done.3
  62.6 0.7 %copy_bitcast_fusion = bf16[32,2,8,128]{3,2,1,0:T(8,128)(2,1)} fusion(bf16[2,32,8,128]{3,2,1,0:T(8,128)(2,1)S(1)} %bitcast.20), kind=kLoop, calls=%fused_computation | loop fusion | bytes 262144 | tf_op jit(solution)/shard_map/transpose | solution.py:479
  63.3 2.0 %shard_map.85 = (f32[8,32,64]{2,1,0:T(8,128)}, f32[27,32,128]{2,1,0:T(8,128)}, f32[27,32,128]{2,1,0:T(8,128)}) custom-call(bf16[16,32,128]{2,1,0:T(8,128)(2,1)} %copy-done.2, bf16[12,32,128]{2,1,0:T(8,128)(2,1)} %copy-done.4, bf16[16,32,128]{2,1,0:T(8,128)(2,1)} %copy-done.3, bf16[12,32,128]{2,1,0:T(8,128)(2,1)} %copy-done.5, bf16[4,32,128]{2,1,0:T(8,128)(2,1)} %copy-done.7), custom_call_target="tpu_custom_call" | custom-call | tf_op jit(solution)/shard_map/pallas_call | solution.py:480
  (2 shorter events, 0.0 us)
Async XLA Ops:
  0.6 1.1 %copy-start.8 = (bf16[64,4,4,256]{3,2,1,0:T(4,128)(2,1)S(1)}, bf16[64,4,4,256]{3,2,1,0:T(4,128)(2,1)}, u32[]{:S(2)}) copy-start(bf16[64,4,4,256]{3,2,1,0:T(4,128)(2,1)} %param.5) | copy-start | bytes 1572868
  1.7 0.9 %copy-start = (bf16[27,32,128]{2,1,0:T(8,128)(2,1)S(1)}, bf16[27,32,128]{2,1,0:T(8,128)(2,1)}, u32[]{:S(2)}) copy-start(bf16[27,32,128]{2,1,0:T(8,128)(2,1)} %wm.1) | copy-start | bytes 663556
  1.7 1.0 %copy-start.1 = (bf16[27,32,128]{2,1,0:T(8,128)(2,1)S(1)}, bf16[27,32,128]{2,1,0:T(8,128)(2,1)}, u32[]{:S(2)}) copy-start(bf16[27,32,128]{2,1,0:T(8,128)(2,1)} %wl.1) | copy-start | bytes 663556
  1.7 1.0 %copy-start.6 = (bf16[8,32,64]{2,1,0:T(8,128)(2,1)S(1)}, bf16[8,32,64]{2,1,0:T(8,128)(2,1)}, u32[]{:S(2)}) copy-start(bf16[8,32,64]{2,1,0:T(8,128)(2,1)} %sw.1) | copy-start | bytes 98308
  60.1 0.6 copy-start.4
  60.7 0.6 copy-start.5
  61.3 0.6 copy-start.7
  61.9 0.6 copy-start.2
  61.9 0.7 %copy-start.3 = (bf16[16,32,128]{2,1,0:T(8,128)(2,1)}, bf16[16,32,128]{2,1,0:T(8,128)(2,1)S(1)}, u32[]{:S(2)}) copy-start(bf16[16,32,128]{2,1,0:T(8,128)(2,1)S(1)} %get-tuple-element.16.middle_0) | copy-start | bytes 393220

commit v3 on v2

--- a/solution.py
+++ b/solution.py
@@ -10,7 +10,7 @@
 F32 = jnp.float32
 BF16 = jnp.bfloat16
 MESH = pl.DeviceIdType.MESH
-CHUNKS = (15, 12, 15, 12, 4)
+CHUNKS = (15, 12, 15, 12)
 NEAR = [(z, y) for z in (-1, 0, 1) for y in (-1, 0, 1) if (z, y) != (0, 0)]
 
 
@@ -34,12 +34,13 @@
 ):
     res, *outs = refs[:6]
     SW, WM, WL, XL, XM, XG, XD, U, pre_l, pre_m, R = refs[6:17]
-    bufs = [refs[17 + 6 * i : 23 + 6 * i] for i in range(5)]
+    bufs = [refs[17 + 6 * i : 23 + 6 * i] for i in range(4)]
+    pb_s, zr_s, dr_s = refs[41:44]
     (
     near_send, near_recv, swap_send, swap_recv,
     wz_send, wz_recv, wg_send, wg_recv, wp_send, wp_recv,
-    s1_send, s1_recv, s2_send, s2_recv, s3_send, s3_recv, s4_send, s4_recv, s5_send, s5_recv,
-    ) = refs[47:]
+    s1_send, s1_recv, s2_send, s2_recv, s3_send, s3_recv, s4_send, s4_recv,
+    ) = refs[44:]
     d, f = lax.axis_index("depth"), lax.axis_index("filt")
     oc, C = cot.shape[1], WM.shape[1]
     CI = up.shape[1]
@@ -52,7 +53,7 @@
 
     for X in (XL, XM, XG, XD):
         X[...] = jnp.zeros_like(X)
-    for X, used in ((WM, T), (WL, T), *((bufs[i][0], CHUNKS[i]) for i in range(5))):
+    for X, used in ((WM, T), (WL, T), *((bufs[i][0], CHUNKS[i]) for i in range(4))):
         if X.shape[0] > used:
             X[used:] = jnp.zeros((X.shape[0] - used,) + X.shape[1:], X.dtype)
     own = pl.ds(pl.multiple_of(f * oc, oc), oc)
@@ -66,7 +67,7 @@
 
     barrier = pltpu.get_barrier_semaphore()
     greet = [(0, k) for k in range(1, m)] + [(y, z) for z, y in NEAR if y != 0]
-    greet += [(2 * j, 0) for j in range(1, n // 2)]
+    greet += [(j, 0) for j in range(2, n - 1)]
     for step in greet:
         pl.semaphore_signal(barrier, inc=1, device_id=at(*step), device_id_type=MESH)
     pl.semaphore_wait(barrier, len(greet))
@@ -100,6 +101,19 @@
         return copies
 
     wm_copies = weight_out(0, WM)
+    wl_copies = weight_out(1, WL)
+    cot_copies = []
+    for k in range(1, m):
+        where = at(0, k)
+        copy = remote(
+            cot.at[:, :, pl.ds(mul(where[1], cols), cols)],
+            XG.at[pl.ds(1, dl), own, pl.ds(W, cols)],
+            swap_send.at[1, k - 1],
+            swap_recv.at[1, k - 1],
+            where,
+        )
+        copy.start()
+        cot_copies.append(copy)
     XG[pl.ds(1, dl), own, pl.ds(W, cols)] = cot[:, :, pl.ds(mul(f, cols), cols)]
 
     line = lax.broadcasted_iota(jnp.int32, (2 * W, 2 * W), 0)
@@ -203,11 +217,8 @@
     def sum_2(index, copies, pb, r1, z, pr):
         copies[0].wait()
 
-        def body(t, carry):
+        for t in range(pb.shape[0]):
             z[t] = (pb[t, :, half].astype(F32) + r1[t].astype(F32)).astype(BF16)
-            return carry
-
-        lax.fori_loop(0, pb.shape[0], body, 0)
         share = pb.shape[0] // groups
         out = []
         for j in range(1, groups):
@@ -228,14 +239,11 @@
             copy.wait()
         share = y.shape[0]
 
-        def body(t, carry):
+        for t in range(share):
             total = z[slot * share + t].astype(F32)
             for j in range(groups - 1):
                 total += pr[j, t].astype(F32)
             y[t] = total.astype(BF16)
-            return carry
-
-        lax.fori_loop(0, share, body, 0)
         out = []
         for k in range(1, m):
             where = at(0, k)
@@ -252,29 +260,49 @@
         share = y.shape[0]
         part = pl.ds(mul(half, hb), hb)
 
-        def body(t, carry):
+        for t in range(share):
             total = y[t, f].astype(F32)
             for k in range(m - 1):
                 total += zr[k, t].astype(F32)
             out[slot * share + t, part, :] = total.astype(BF16)
-            return carry
-
-        lax.fori_loop(0, share, body, 0)
         piece = out.at[pl.ds(slot * share, share), part]
         copies = []
-        for j in range(1, groups):
-            copy = remote(piece, piece, s4_send.at[index, j - 1], s4_recv.at[index, j - 1], at(2 * j, 0))
+        for j in range(1, n):
+            copy = remote(piece, piece, s4_send.at[index, j - 1], s4_recv.at[index, j - 1], at(j, 0))
             copy.start()
             copies.append(copy)
         return copies
 
-    def sum_5(index, copies, out):
+    def stride_1():
+        copies = []
+        for k in range(1, m):
+            where = at(0, k)
+            copy = remote(pb_s.at[where[1]], zr_s.at[k - 1], s3_send.at[4, k - 1], s3_recv.at[4, k - 1], where)
+            copy.start()
+            copies.append(copy)
+        return copies
+
+    def stride_2(copies):
         for copy in copies:
             copy.wait()
-        part = pl.ds(mul(half, hb), hb)
-        copy = remote(out.at[:, part], out.at[:, part], s5_send.at[index], s5_recv.at[index], (mate, f))
-        copy.start()
-        return [copy]
+        total = pb_s[f].astype(F32)
+        for k in range(m - 1):
+            total += zr_s[k].astype(F32)
+        dr_s[d] = total.astype(BF16)
+        copies = []
+        for j in range(1, n):
+            copy = remote(dr_s.at[d], dr_s.at[d], s4_send.at[4, j - 1], s4_recv.at[4, j - 1], at(j, 0))
+            copy.start()
+            copies.append(copy)
+        return copies
+
+    def stride_3(copies):
+        for copy in copies:
+            copy.wait()
+        total = dr_s[0].astype(F32)
+        for j in range(1, n):
+            total += dr_s[j].astype(F32)
+        outs[4][...] = total
 
     def weight_spread(index, copies, dst):
         share = dst.shape[0] // groups
@@ -308,19 +336,6 @@
         pre_l[plane] = value
         XL[plane + 1, :, W : W + cols] = silu(value).astype(BF16)
     near_start(0, XL)
-    wl_copies = weight_out(1, WL)
-    cot_copies = []
-    for k in range(1, m):
-        where = at(0, k)
-        copy = remote(
-            cot.at[:, :, pl.ds(mul(where[1], cols), cols)],
-            XG.at[pl.ds(1, dl), own, pl.ds(W, cols)],
-            swap_send.at[1, k - 1],
-            swap_recv.at[1, k - 1],
-            where,
-        )
-        copy.start()
-        cot_copies.append(copy)
     wm_pass = weight_spread(0, wm_copies, WM)
     wm_pass = weight_pass(0, wm_pass, WM)
     wl_pass = weight_spread(1, wl_copies, WL)
@@ -355,10 +370,8 @@
             going[index] = sum_2(index, going[index], pb, r1, z, pr)
         elif number == 3:
             going[index] = sum_3(index, going[index], z, pr, y, zr)
-        elif number == 4:
+        else:
             going[index] = sum_4(index, going[index], y, zr, outs[index])
-        else:
-            going[index] = sum_5(index, going[index], outs[index])
 
     left = grad_left(XG)
     weight_grad(left, XM, bufs[0][0], range(5))
@@ -380,12 +393,11 @@
     total = dot(left[0], U[:, :cols], (1, 1))
     for plane in range(1, dl):
         total += dot(left[plane], U[:, plane * cols : (plane + 1) * cols], (1, 1))
-    total = total.astype(BF16)
-    for pair in range(4):
-        bufs[4][0][pair] = total[:, pair * 2 * CI : (pair + 1) * 2 * CI].reshape(bufs[4][0].shape[1:])
-    step(1, 4)
-    for number, index in ((2, 2), (2, 3), (2, 4), (3, 0), (3, 1)):
+    pb_s[...] = total.astype(BF16).reshape(pb_s.shape)
+    stride = stride_1()
+    for number, index in ((2, 2), (2, 3), (3, 0), (3, 1)):
         step(number, index)
+    stride = stride_2(stride)
 
     for plane in range(dl):
         R[plane] = conv(XM, WL, plane).astype(BF16)
@@ -404,10 +416,9 @@
         out_copies.append(copy)
     res[:, :, out_spot] = R[:, own]
 
-    for number, index in (
-        (3, 2), (4, 0), (3, 3), (4, 1), (3, 4), (5, 0), (4, 2), (5, 1), (4, 3), (4, 4), (5, 2), (5, 3), (5, 4)
-    ):
+    for number, index in ((3, 2), (3, 3), (4, 0), (4, 1), (4, 2), (4, 3)):
         step(number, index)
+    stride_3(stride)
     for copy in out_copies + [copy for copies in going.values() for copy in copies]:
         copy.wait()
     for index, X in enumerate((XL, XG, XM, XD)):
@@ -427,7 +438,6 @@
     groups = n // 2
     TP = -(-T // groups) * groups
     sizes = [-(-count // groups) * groups for count in CHUNKS]
-    lanes = [C] * 4 + [2 * CI]
 
     def sums(count, lanes):
         share = count // groups
@@ -447,7 +457,8 @@
         functools.partial(kernel, n, m, dl, hl, W),
         out_shape=(
             jax.ShapeDtypeStruct((dl, oc, H * W), BF16),
-            *(jax.ShapeDtypeStruct((size, oc, wide_), BF16) for size, wide_ in zip(sizes, lanes)),
+            *(jax.ShapeDtypeStruct((size, oc, C), BF16) for size in sizes),
+            jax.ShapeDtypeStruct((oc, 8 * CI), F32),
         ),
         in_specs=[pl.BlockSpec(memory_space=pltpu.VMEM)] * 5,
         out_specs=[pl.BlockSpec(memory_space=pltpu.VMEM)] * 6,
@@ -460,17 +471,19 @@
             pltpu.VMEM((dl, C, hl * W), F32),
             pltpu.VMEM((dl, C, hl * W), F32),
             pltpu.VMEM((dl, C, hl * W), BF16),
-            *(buf for size, wide_ in zip(sizes, lanes) for buf in sums(size, wide_)),
+            *(buf for size in sizes for buf in sums(size, C)),
+            pltpu.VMEM((m, oc, 8 * CI), BF16),
+            pltpu.VMEM((m - 1, oc, 8 * CI), BF16),
+            pltpu.VMEM((n, oc, 8 * CI), BF16),
             *sems(4, 8),
             *sems(3, m - 1),
             *sems(2, m - 1),
             *sems(2, m - 1, groups - 1),
             *sems(2, m - 1),
-            *sems(5),
-            *sems(5, groups - 1),
+            *sems(4),
+            *sems(4, groups - 1),
             *sems(5, m - 1),
-            *sems(5, groups - 1),
-            *sems(5),
+            *sems(5, n - 1),
         ],
         compiler_params=pltpu.CompilerParams(
             collective_id=0, has_side_effects=True, vmem_limit_bytes=52 * 1024 * 1024
@@ -498,7 +511,7 @@
         target[start : start + count] = source[:count].astype(F32)
     CI = gs.shape[2]
     for tap in range(8):
-        gs[tap] = stride[tap // 2].astype(F32)[:, (tap % 2) * CI : (tap % 2 + 1) * CI]
+        gs[tap] = stride[:, tap * CI : (tap + 1) * CI]
 
 
 def solution(mesh):

time: 65.5 us -> 64.8 us (0.989)
  Pallas kernels: 59.3 us -> 58.5 us
    pallas_call x1, Pallas kernels: 57.3 us -> 56.5 us  [per_device(): pl.pallas_call(functools.partial(kernel, n, m, dl, hl, W), out_shape=(jax...]
where the time goes in v3:
time: 64.8 us; the launch traced here: 64.6 us
  Pallas kernels  58.5 us (90%)
  local copies, waits for them, and re-layouts  5.4 us (8%)
  between operations  0.68 us (1%)
    pallas_call x1, Pallas kernels, per_device(): pl.pallas_call(functools.partial(kernel, n, m, dl, hl, W), out_shape=(jax...  56.5 us
    unnamed x19, local copies, waits for them, and re-layouts  3.54 us
    pallas_call x1, Pallas kernels, per_device(): pl.pallas_call(widen, out_shape=(jax.ShapeDtypeStruct((8, oc, CI), F32),...  2.04 us

profile of v3, /device:TPU:0, one launch (start us, length us, event | category | flops | bytes accessed | tf_op | source)
XLA Modules:
  0.0 64.6 jit_solution(17499889571771553418)
XLA Ops:
  0.6 0.0 copy-start.8
  0.6 1.0 %reshape.20 = bf16[2,32,1024]{2,0,1:T(2,128)(2,1)S(1)} reshape(bf16[2,32,8,128]{3,2,0,1:T(8,128)(2,1)} %bitcast.21) | data formatting | bytes 262144 | tf_op jit(solution)/shard_map/reshape | solution.py:435
  1.7 0.1 copy-done.8
  1.7 0.0 copy-start
  1.7 0.0 copy-start.1
  1.7 0.0 copy-start.6
  1.7 0.2 copy.9
  1.9 0.8 %copy-done = bf16[27,32,128]{2,1,0:T(8,128)(2,1)S(1)} copy-done((bf16[27,32,128]{2,1,0:T(8,128)(2,1)S(1)}, bf16[27,32,128]{2,1,0:T(8,128)(2,1)}, u32[]{:S(2)}) %copy-start) | copy-done | bytes 221208
  2.7 0.1 copy-done.1
  2.8 0.0 copy-done.6
  2.8 56.5 %shard_map.84 = (bf16[2,32,1024]{2,1,0:T(8,128)(2,1)S(1)}, bf16[16,32,128]{2,1,0:T(8,128)(2,1)S(1)}, bf16[12,32,128]{2,1,0:T(8,128)(2,1)S(1)}, bf16[16,32,128]{2...) custom-call(bf16[16,64,256]{2,1,0:T(8,128)(2,1)S(1)} %bitcast.17, ...), custom_call_target="tpu_custom_call" | custom-call | tf_op jit(solution)/shard_map/pallas_call | solution.py:456
  59.3 0.0 copy-start.4
  59.3 0.6 copy-done.4
  59.9 0.0 copy-start.5
  59.9 0.6 copy-done.5
  60.6 0.0 copy-start.7
  60.6 0.6 copy-done.7
  61.2 0.0 copy-start.2
  61.2 0.0 copy-start.3
  61.2 0.6 copy-done.2
  61.8 0.1 copy-done.3
  61.9 0.7 %copy_bitcast_fusion = bf16[32,2,8,128]{3,2,1,0:T(8,128)(2,1)} fusion(bf16[2,32,8,128]{3,2,1,0:T(8,128)(2,1)S(1)} %bitcast.20), kind=kLoop, calls=%fused_computation | loop fusion | bytes 262144 | tf_op jit(solution)/shard_map/transpose | solution.py:492
  62.6 2.0 %shard_map.85 = (f32[8,32,64]{2,1,0:T(8,128)}, f32[27,32,128]{2,1,0:T(8,128)}, f32[27,32,128]{2,1,0:T(8,128)}) custom-call(bf16[16,32,128]{2,1,0:T(8,128)(2,1)} %copy-done.2, bf16[12,32,128]{2,1,0:T(8,128)(2,1)} %copy-done.4, bf16[16,32,128]{2,1,0:T(8,128)(2,1)} %copy-done.3, bf16[12,32,128]{2,1,0:T(8,128)(2,1)} %copy-done.5, f32[32,512]{1,0:T(8,128)} %copy-done.7), custom_call_target="tpu_custom_call" | custom-call | tf_op jit(solution)/shard_map/pallas_call | solution.py:493
  (2 shorter events, 0.0 us)
Async XLA Ops:
  0.6 1.1 %copy-start.8 = (bf16[64,4,4,256]{3,2,1,0:T(4,128)(2,1)S(1)}, bf16[64,4,4,256]{3,2,1,0:T(4,128)(2,1)}, u32[]{:S(2)}) copy-start(bf16[64,4,4,256]{3,2,1,0:T(4,128)(2,1)} %param.5) | copy-start | bytes 1572868
  1.7 0.9 %copy-start = (bf16[27,32,128]{2,1,0:T(8,128)(2,1)S(1)}, bf16[27,32,128]{2,1,0:T(8,128)(2,1)}, u32[]{:S(2)}) copy-start(bf16[27,32,128]{2,1,0:T(8,128)(2,1)} %wm.1) | copy-start | bytes 663556
  1.7 1.0 %copy-start.1 = (bf16[27,32,128]{2,1,0:T(8,128)(2,1)S(1)}, bf16[27,32,128]{2,1,0:T(8,128)(2,1)}, u32[]{:S(2)}) copy-start(bf16[27,32,128]{2,1,0:T(8,128)(2,1)} %wl.1) | copy-start | bytes 663556
  1.7 1.0 %copy-start.6 = (bf16[8,32,64]{2,1,0:T(8,128)(2,1)S(1)}, bf16[8,32,64]{2,1,0:T(8,128)(2,1)}, u32[]{:S(2)}) copy-start(bf16[8,32,64]{2,1,0:T(8,128)(2,1)} %sw.1) | copy-start | bytes 98308
  59.3 0.6 copy-start.4
  59.9 0.6 copy-start.5
  60.6 0.6 copy-start.7
  61.2 0.6 copy-start.2
  61.2 0.7 %copy-start.3 = (bf16[16,32,128]{2,1,0:T(8,128)(2,1)}, bf16[16,32,128]{2,1,0:T(8,128)(2,1)S(1)}, u32[]{:S(2)}) copy-start(bf16[16,32,128]{2,1,0:T(8,128)(2,1)S(1)} %get-tuple-element.16.middle_0) | copy-start | bytes 393220
